TPU v7x, 512 devices: a whole 4x8x8 slice. The times are simulated.
512 devices in a mesh: dp: 64 (over y, x, core), mp: 8 (over z).
Axes of the slice: x: 4, y: 8, z: 8, core: 2. Of those that a mesh axis runs over, the one named last changes fastest.
Arguments:
- partial_grads: bfloat16 [64, 2, 2, 512, 4096], P('dp', None, None, None, 'mp')
- factors: bfloat16 [8, 8, 512, 1024], P('mp', None, 'dp'), as said below
- inverse_factors: bfloat16 [8, 8, 512, 1024], P('mp', None, 'dp'), as said below
- probes: bfloat16 [8, 8, 512, 512], P('mp', None, 'dp'), may hold values from -6 to 6
- slot_table: int32 [8, 4], P('mp'), may hold values from 0 to 7, as said below
Outputs:
- preconditioned: bfloat16 [2, 2, 512, 4096], P(None, None, 'dp', 'mp')
- new_factors: bfloat16 [8, 8, 512, 1024], P('mp', None, 'dp')
Inputs may be any that keep to these rules, and one draw needn't show every extreme that they name: `slot_table`: in each row the 4 entries are distinct slots; slot j belongs to owner j // 2 (an owner is a group of 16 consecutive dp devices; the starting program sends slots 2k and 2k+1 to dp device 16k for updating), and in every row some owner holds 2 blocks. `factors`: both halves of every slot are upper triangular with a positive diagonal. `inverse_factors`: both halves of every slot are upper triangular with a positive diagonal.
All inputs are finite; a program needn't handle non-finite values. Where the computation divides by a largest or mean magnitude, that divisor is 1e-20 or more.
Results may differ from a plain program's by a relative error of at most 0.011.
Values may be sent and summed in bfloat16 or wider, within the bound.
A program may use at most 64 MiB of HBM per device.

v0:
```python
import math
import jax
import jax.numpy as jnp
import numpy as np
from jax import lax
from jax.sharding import PartitionSpec as P

GROUP = 16
CLIP_RMS = 0.3
LEARN_RATE = 0.1
EPS_NORM = 1e-06


def product(left_op, right_op):
    return jnp.dot(left_op, right_op, preferred_element_type=jnp.float32)


def step_factor(factor, first_gram, second_gram):
    bound_value = jnp.max(jnp.abs(first_gram + second_gram)) + EPS_NORM
    change = jnp.triu(first_gram - second_gram).astype(jnp.bfloat16)
    moved_rows = product(change, factor)
    return (factor.astype(jnp.float32) - LEARN_RATE / bound_value * moved_rows).astype(jnp.bfloat16)


def update_block(gradient, left_q, right_q, left_inv, right_inv, probe_mat):
    left_times = product(left_q, gradient).astype(jnp.bfloat16)
    whitened = product(left_times, right_q.T).astype(jnp.bfloat16)
    half_conjugate = product(left_inv.T, probe_mat).astype(jnp.bfloat16)
    conjugate = product(half_conjugate, right_inv).astype(jnp.bfloat16)
    new_left = step_factor(left_q, product(whitened, whitened.T), product(conjugate, conjugate.T))
    new_right = step_factor(right_q, product(whitened.T, whitened), product(conjugate.T, conjugate))
    precond_left = product(new_left.T, new_left).astype(jnp.bfloat16)
    precond_right = product(new_right.T, new_right).astype(jnp.bfloat16)
    middle = product(precond_left, gradient).astype(jnp.bfloat16)
    result = product(middle, precond_right).astype(jnp.bfloat16)
    return (result, jnp.concatenate([new_left, new_right], axis=1))


def pick_slots(onehot, source):
    return jnp.einsum("bj,jrc->brc", onehot, source, preferred_element_type=jnp.float32).astype(
        jnp.bfloat16
    )


def place_slots(onehot, source):
    return jnp.einsum("bj,brc->jrc", onehot, source, preferred_element_type=jnp.float32).astype(
        jnp.bfloat16
    )


def body(partial_grads, factors, inverse_factors, probes, slot_table):
    devices = lax.axis_size("dp")
    my_index = lax.axis_index("dp")
    local_sum = partial_grads[0].astype(jnp.float32)
    experts, block_rows, block_size, columns = local_sum.shape
    summed = lax.psum_scatter(local_sum, "dp", scatter_dimension=2, tiled=True)
    rows_dev = summed.shape[2]
    blocks_col = experts * block_rows
    gradient = summed.reshape(blocks_col, rows_dev, columns)
    entry_count = blocks_col * block_size * columns * lax.axis_size("mp")
    squares = lax.psum(jnp.sum(gradient * gradient), ("dp", "mp"))
    clip_factor = jnp.minimum(1.0, CLIP_RMS * math.sqrt(entry_count) / jnp.sqrt(squares + EPS_NORM))
    clipped = (gradient * clip_factor).astype(jnp.bfloat16)
    old_state = factors[0]
    combined_state = jnp.concatenate([old_state, inverse_factors[0]], axis=2)
    probe_rows = probes[0]
    own_slots = old_state.shape[0]
    slot_row = slot_table[0]
    onehot = (slot_row[:, None] == jnp.arange(own_slots, dtype=jnp.int32)[None, :]).astype(
        jnp.bfloat16
    )
    occupied = jnp.sum(onehot.astype(jnp.float32), axis=0) > 0.5
    slots_dev = own_slots // (devices // GROUP)
    target = np.arange(own_slots) // slots_dev * GROUP
    position = np.arange(own_slots) % slots_dev
    unit_grad = place_slots(onehot, clipped)
    global_rows = my_index * rows_dev + jnp.arange(rows_dev, dtype=jnp.int32)
    diagonal = (jnp.arange(columns, dtype=jnp.int32)[None, :] == global_rows[:, None]).astype(
        jnp.bfloat16
    )
    filler = jnp.concatenate([diagonal, diagonal, diagonal, diagonal], axis=1)
    send_grad = (
        jnp.zeros((devices, slots_dev, rows_dev, columns), jnp.bfloat16)
        .at[target, position]
        .set(unit_grad)
    )
    send_state = (
        jnp.broadcast_to(filler, (devices, slots_dev, rows_dev, 4 * columns))
        .at[target, position]
        .set(combined_state)
    )
    send_probe = (
        jnp.zeros((devices, slots_dev, rows_dev, columns), jnp.bfloat16)
        .at[target, position]
        .set(probe_rows)
    )
    grad_in = lax.all_to_all(send_grad, "dp", split_axis=0, concat_axis=2, tiled=True)
    state_in = lax.all_to_all(send_state, "dp", split_axis=0, concat_axis=2, tiled=True)
    probe_in = lax.all_to_all(send_probe, "dp", split_axis=0, concat_axis=2, tiled=True)

    def run_one(item_set):
        state = item_set[1]
        return update_block(
            item_set[0],
            state[:, :block_size],
            state[:, block_size : 2 * block_size],
            state[:, 2 * block_size : 3 * block_size],
            state[:, 3 * block_size :],
            item_set[2],
        )

    result, moved_rows = lax.map(run_one, (grad_in[0], state_in[0], probe_in[0]))
    back_grad = lax.all_to_all(result[None], "dp", split_axis=2, concat_axis=0, tiled=True)
    back_state = lax.all_to_all(moved_rows[None], "dp", split_axis=2, concat_axis=0, tiled=True)
    unit_back = back_grad[target, position]
    state_back = back_state[target, position]
    precond = pick_slots(onehot, unit_back)
    new_state = jnp.where(occupied[:, None, None], state_back, old_state)
    return (precond.reshape(experts, block_rows, rows_dev, columns), new_state[None])


def solution(mesh):
    return jax.shard_map(
        body,
        mesh=mesh,
        in_specs=(
            P("dp", None, None, None, "mp"),
            P("mp", None, "dp", None),
            P("mp", None, "dp", None),
            P("mp", None, "dp", None),
            P("mp", None),
        ),
        out_specs=(P(None, None, "dp", "mp"), P("mp", None, "dp", None)),
        check_vma=False,
    )
```

profile of v0, /device:TPU:2, one launch (start us, length us, event | category | flops | bytes accessed | tf_op | source)
XLA Modules:
  0.0 513.9 jit_solution(15969105971914788014)
XLA Ops:
  8.3 2.3 scatter_fusion.2
  10.6 10.7 %all-to-all-start.2 = ((bf16[64,2,8,512]{3,2,1,0:T(8,128)(2,1)}), bf16[64,2,8,512]{3,2,1,0:T(8,128)(2,1)S(1)}, u32[]{:S(2)}, u32[]{:S(2)}) async-start(bf16[64,2,8,512]{3,2,1,0:T(8,128)(2,1)} %scatter_fusion.2), calls=%async_computation.3 | async-start | bytes 2097152 | tf_op jit(solution)/shard_map/all_to_all | solution.py:99
  21.4 2.5 broadcast_in_dim.73
  26.1 23.9 %all-to-all-done.2 = bf16[64,2,8,512]{3,2,1,0:T(8,128)(2,1)S(1)} async-done(((bf16[64,2,8,512]{3,2,1,0:T(8,128)(2,1)}), bf16[64,2,8,512]{3,2,1,0:T(8,128)(2,1)S(1)}, u32[]{:S(2)}, u32[]{:S(2)}) %all-to-all-start.2) | async-done | bytes 1048608 | tf_op jit(solution)/shard_map/all_to_all | solution.py:99
  50.0 5.8 %all-to-all-start = ((bf16[64,2,8,2048]{3,2,1,0:T(8,128)(2,1)}), bf16[64,2,8,2048]{3,2,1,0:T(8,128)(2,1)}, u32[]{:S(2)}, u32[]{:S(2)}) async-start(bf16[64,2,8,2048]{3,2,1,0:T(8,128)(2,1)} %scatter_fusion), calls=%async_computation | async-start | bytes 8388608 | tf_op jit(solution)/shard_map/all_to_all | solution.py:98
  55.9 2.5 bitcast_convert_fusion
  58.5 158.2 %reduce-scatter.2.cloned.1.call-done = f32[2,2,8,512]{3,2,1,0:T(8,128)} async-done(((f32[2,2,512,512]{3,2,1,0:T(8,128)}), f32[2,2,8,512]{3,2,1,0:T(8,128)}) %reduce-scatter.2.cloned.1.call-update) | async-done | bytes 65552 | tf_op jit(solution)/shard_map/reduce_scatter | solution.py:56
  218.2 97.7 %psum.7 = f32[]{:T(128)} all-reduce(f32[]{:T(128)} %multiply_reduce_fusion), channel_id=1, replica_groups=mesh['dp'=64,'mp'=8] {'dp','mp'}, use_global_device_ids=true, to_apply=%region_2.0 | all-reduce | flops 1 | bytes 8 | tf_op jit(solution)/shard_map/psum | solution.py:61
  320.8 8.5 %all-to-all-start.1 = ((bf16[64,2,8,512]{3,2,1,0:T(8,128)(2,1)}), bf16[64,2,8,512]{3,2,1,0:T(8,128)(2,1)S(1)}, u32[]{:S(2)}, u32[]{:S(2)}) async-start(bf16[64,2,8,512]{3,2,1,0:T(8,128)(2,1)} %scatter_fusion.1), calls=%async_computation.2 | async-start | bytes 2097152 | tf_op jit(solution)/shard_map/all_to_all | solution.py:97
  329.4 4.7 copy_bitcast_fusion
  334.1 24.0 %all-to-all-done.1 = bf16[64,2,8,512]{3,2,1,0:T(8,128)(2,1)S(1)} async-done(((bf16[64,2,8,512]{3,2,1,0:T(8,128)(2,1)}), bf16[64,2,8,512]{3,2,1,0:T(8,128)(2,1)S(1)}, u32[]{:S(2)}, u32[]{:S(2)}) %all-to-all-start.1) | async-done | bytes 1048608 | tf_op jit(solution)/shard_map/all_to_all | solution.py:97
  359.2 48.4 %while.12 = (s32[]{:T(128)}, bf16[2,512,512]{2,1,0:T(8,128)(2,1)}, bf16[2,512,1024]{1,2,0:T(8,128)(2,1)}, bf16[2,512,2048]{2,1,0:T(8,128)(2,1)}, bf16[2,512,512]...) while((s32[]{:T(128)}, bf16[2,512,512]{2,1,0:T(8,128)(2,1)}, ...), condition=%wide.region_9.10_spmd, body=%wide.region_6.9_spmd.sunk | while | flops 3768058368 | bytes 53485872 | solution.py:112
  361.3 2.5 copy.74
  370.7 2.6 fusion.115
  380.6 2.8 fusion.116
  385.5 2.5 copy.74
  394.9 2.6 fusion.115
  404.8 2.7 fusion.116
  407.6 3.3 copy.72
  410.9 5.6 %all-to-all-start.3 = ((bf16[1,2,512,512]{3,1,0,2:T(2,128)(2,1)}), bf16[1,2,512,512]{3,1,0,2:T(2,128)(2,1)S(1)}, u32[]{:S(2)}, u32[]{:S(2)}) async-start(bf16[1,2,512,512]{3,1,0,2:T(2,128)(2,1)} %bitcast.83), calls=%async_computation.4 | async-start | bytes 2097152 | tf_op jit(solution)/shard_map/all_to_all | solution.py:113
  416.5 6.3 %copy.50 = bf16[2,512,1024]{2,0,1:T(2,128)(2,1)} copy(bf16[2,512,1024]{1,2,0:T(8,128)(2,1)} %get-tuple-element.36) | data formatting | bytes 4194304 | tf_op jit(solution)/shard_map/while | solution.py:112
  422.8 22.5 %all-to-all-done.3 = bf16[1,2,512,512]{3,1,0,2:T(2,128)(2,1)S(1)} async-done(((bf16[1,2,512,512]{3,1,0,2:T(2,128)(2,1)}), bf16[1,2,512,512]{3,1,0,2:T(2,128)(2,1)S(1)}, u32[]{:S(2)}, u32[]{:S(2)}) %all-to-all-start.3) | async-done | bytes 1048608 | tf_op jit(solution)/shard_map/all_to_all | solution.py:113
  445.3 5.7 %all-to-all-start.4 = ((bf16[1,2,512,1024]{3,1,0,2:T(2,128)(2,1)}), bf16[1,2,512,1024]{3,1,0,2:T(2,128)(2,1)S(1)}, u32[]{:S(2)}, u32[]{:S(2)}) async-start(bf16[1,2,512,1024]{3,1,0,2:T(2,128)(2,1)} %bitcast.26), calls=%async_computation.5 | async-start | bytes 4194304 | tf_op jit(solution)/shard_map/all_to_all | solution.py:114
  455.0 47.3 %all-to-all-done.4 = bf16[1,2,512,1024]{3,1,0,2:T(2,128)(2,1)S(1)} async-done(((bf16[1,2,512,1024]{3,1,0,2:T(2,128)(2,1)}), bf16[1,2,512,1024]{3,1,0,2:T(2,128)(2,1)S(1)}, u32[]{:S(2)}, u32[]{:S(2)}) %all-to-all-start.4) | async-done | bytes 2097184 | tf_op jit(solution)/shard_map/all_to_all | solution.py:114
  (80 shorter events, 48.9 us)
Async XLA Ops:
  7.2 14.2 %copy-start.7 = (bf16[1,8,8,1024]{3,2,1,0:T(8,128)(2,1)S(1)}, bf16[1,8,8,1024]{3,2,1,0:T(8,128)(2,1)}, u32[]{:S(2)}) copy-start(bf16[1,8,8,1024]{3,2,1,0:T(8,128)(2,1)} %param.20) | copy-start | bytes 393220
  7.2 14.2 %copy-start.8 = (bf16[1,8,8,1024]{3,2,1,0:T(8,128)(2,1)S(1)}, bf16[1,8,8,1024]{3,2,1,0:T(8,128)(2,1)}, u32[]{:S(2)}) copy-start(bf16[1,8,8,1024]{3,2,1,0:T(8,128)(2,1)} %param.21) | copy-start | bytes 393220
  10.6 39.5 %all-to-all-start.2 = ((bf16[64,2,8,512]{3,2,1,0:T(8,128)(2,1)}), bf16[64,2,8,512]{3,2,1,0:T(8,128)(2,1)S(1)}, u32[]{:S(2)}, u32[]{:S(2)}) async-start(bf16[64,2,8,512]{3,2,1,0:T(8,128)(2,1)} %scatter_fusion.2), calls=%async_computation.3 | async-start | bytes 2097152 | tf_op jit(solution)/shard_map/all_to_all | solution.py:99
  21.4 2.5 copy-start.6
  26.1 29.8 %copy-start.1 = (bf16[1,2,2,512,512]{4,3,2,1,0:T(8,128)(2,1)S(1)}, bf16[1,2,2,512,512]{4,3,2,1,0:T(8,128)(2,1)}, u32[]{:S(2)}) copy-start(bf16[1,2,2,512,512]{4,3,2,1,0:T(8,128)(2,1)} %param.19) | copy-start | bytes 6291460
  50.0 270.8 %all-to-all-start = ((bf16[64,2,8,2048]{3,2,1,0:T(8,128)(2,1)}), bf16[64,2,8,2048]{3,2,1,0:T(8,128)(2,1)}, u32[]{:S(2)}, u32[]{:S(2)}) async-start(bf16[64,2,8,2048]{3,2,1,0:T(8,128)(2,1)} %scatter_fusion), calls=%async_computation | async-start | bytes 8388608 | tf_op jit(solution)/shard_map/all_to_all | solution.py:98
  55.9 160.8 %reduce-scatter.2.cloned.1.call-start = ((), (), s32[]{:S(2)}) async-start(), calls=%async_computation.6 | async-start | bytes 4259840 | tf_op jit(solution)/shard_map/reduce_scatter | solution.py:56
  58.5 258.9 %copy-start.9 = (s32[1,4]{1,0:T(1,128)S(1)}, s32[1,4]{1,0:T(1,128)}, u32[]{:S(2)}) copy-start(s32[1,4]{1,0:T(1,128)} %param.23) | copy-start | bytes 52
  320.8 37.3 %all-to-all-start.1 = ((bf16[64,2,8,512]{3,2,1,0:T(8,128)(2,1)}), bf16[64,2,8,512]{3,2,1,0:T(8,128)(2,1)S(1)}, u32[]{:S(2)}, u32[]{:S(2)}) async-start(bf16[64,2,8,512]{3,2,1,0:T(8,128)(2,1)} %scatter_fusion.1), calls=%async_computation.2 | async-start | bytes 2097152 | tf_op jit(solution)/shard_map/all_to_all | solution.py:97
  359.2 4.6 copy-start.2
  365.7 1.2 copy-start.4
  374.9 2.6 copy-start
  377.5 1.6 copy-start.5
  380.6 2.8 copy-start.3
  383.4 4.6 copy-start.2
  389.9 1.2 copy-start.4
  399.1 2.6 copy-start
  401.7 1.6 copy-start.5
  404.8 2.7 copy-start.3
  410.9 34.4 %all-to-all-start.3 = ((bf16[1,2,512,512]{3,1,0,2:T(2,128)(2,1)}), bf16[1,2,512,512]{3,1,0,2:T(2,128)(2,1)S(1)}, u32[]{:S(2)}, u32[]{:S(2)}) async-start(bf16[1,2,512,512]{3,1,0,2:T(2,128)(2,1)} %bitcast.83), calls=%async_computation.4 | async-start | bytes 2097152 | tf_op jit(solution)/shard_map/all_to_all | solution.py:113
  445.3 56.9 %all-to-all-start.4 = ((bf16[1,2,512,1024]{3,1,0,2:T(2,128)(2,1)}), bf16[1,2,512,1024]{3,1,0,2:T(2,128)(2,1)S(1)}, u32[]{:S(2)}, u32[]{:S(2)}) async-start(bf16[1,2,512,1024]{3,1,0,2:T(2,128)(2,1)} %bitcast.26), calls=%async_computation.5 | async-start | bytes 4194304 | tf_op jit(solution)/shard_map/all_to_all | solution.py:114
Sparse Core Ops, SparseCore 0:
  61.4 155.2 reduce-scatter.1
where the time goes:
time: 516 us; the launch traced here: 514 us
  waiting for transfers between devices  276 us (53%)
  blocking collectives  97.7 us (19%)
  local copies, waits for them, and re-layouts  46.2 us (9%)
  starting transfers between devices  36.3 us (7%)
  matrix products  31.9 us (6%)
  between operations  14.9 us (3%)
  other arithmetic  7.96 us (2%)
    reduce_scatter x1, waiting for transfers between devices, body(): summed = lax.psum_scatter(local_sum, 'dp', scatter_dimension=2, tiled=True)  158 us
    psum x1, blocking collectives, body(): squares = lax.psum(jnp.sum(gradient * gradient), ('dp', 'mp'))  97.7 us
    all_to_all x1, waiting for transfers between devices, body(): lax.all_to_all(moved_rows[None], 'dp', split_axis=2, concat_axis=0, tiled...  47.3 us
    dot_general x20, matrix products, product(): return jnp.dot(left_op, right_op, preferred_element_type=jnp.float32)  31.4 us
    all_to_all x1, waiting for transfers between devices, body(): lax.all_to_all(send_grad, 'dp', split_axis=0, concat_axis=2, tiled=True)  24 us
    all_to_all x1, waiting for transfers between devices, body(): lax.all_to_all(send_probe, 'dp', split_axis=0, concat_axis=2, tiled=True)  23.9 us
    all_to_all x1, waiting for transfers between devices, body(): lax.all_to_all(result[None], 'dp', split_axis=2, concat_axis=0, tiled=True)  22.5 us
    all_to_all x1, starting transfers between devices, body(): lax.all_to_all(send_probe, 'dp', split_axis=0, concat_axis=2, tiled=True)  10.7 us
  transfers between devices with their start and end apart: 6, of which 5 were waited for; matrix products, arithmetic and copies ran while one was open for 5% of the time, Pallas kernels for 0%

commit v1 on v0

--- a/solution.py
+++ b/solution.py
@@ -110,7 +110,10 @@
         )
 
     result, moved_rows = lax.map(run_one, (grad_in[0], state_in[0], probe_in[0]))
-    back_grad = lax.all_to_all(result[None], "dp", split_axis=2, concat_axis=0, tiled=True)
+    own = result[None]
+    cells = jnp.split(own, lax.axis_size("dp"), axis=2)
+    received = lax.all_to_all(jnp.stack(cells), "dp", 0, 0)
+    back_grad = jnp.concatenate(received, axis=0)
     back_state = lax.all_to_all(moved_rows[None], "dp", split_axis=2, concat_axis=0, tiled=True)
     unit_back = back_grad[target, position]
     state_back = back_state[target, position]

time: 516 us -> 601 us (1.16)
  local copies, waits for them, and re-layouts: 46.2 us -> 127 us
    unnamed x11 -> x74, local copies, waits for them, and re-layouts: 0.65 us -> 83.6 us
  transfers between devices with their start and end apart: 6 -> 6, of which waited for: 5 -> 5; matrix products, arithmetic and copies ran while one was open for 5% -> 4% of each run, Pallas kernels for 0% -> 0%
where the time goes in v1:
time: 601 us; the launch traced here: 596 us
  waiting for transfers between devices  278 us (46%)
  local copies, waits for them, and re-layouts  127 us (21%)
  blocking collectives  97.7 us (16%)
  starting transfers between devices  36.6 us (6%)
  matrix products  30.4 us (5%)
  between operations  14.9 us (2%)
  other arithmetic  7.93 us (1%)
    reduce_scatter x1, waiting for transfers between devices, body(): summed = lax.psum_scatter(local_sum, 'dp', scatter_dimension=2, tiled=True)  158 us
    psum x1, blocking collectives, body(): squares = lax.psum(jnp.sum(gradient * gradient), ('dp', 'mp'))  97.7 us
    unnamed x74, local copies, waits for them, and re-layouts  83.6 us
    all_to_all x1, waiting for transfers between devices, body(): lax.all_to_all(moved_rows[None], 'dp', split_axis=2, concat_axis=0, tiled...  49.8 us
    dot_general x20, matrix products, product(): return jnp.dot(left_op, right_op, preferred_element_type=jnp.float32)  29.9 us
    all_to_all x1, waiting for transfers between devices, body(): lax.all_to_all(send_grad, 'dp', split_axis=0, concat_axis=2, tiled=True)  24 us
    all_to_all x1, waiting for transfers between devices, body(): lax.all_to_all(send_probe, 'dp', split_axis=0, concat_axis=2, tiled=True)  23.9 us
    all_to_all x1, waiting for transfers between devices, body(): received = lax.all_to_all(jnp.stack(cells), 'dp', 0, 0)  22.5 us
  transfers between devices with their start and end apart: 6, of which 5 were waited for; matrix products, arithmetic and copies ran while one was open for 4% of the time, Pallas kernels for 0%

profile of v1, /device:TPU:2, one launch (start us, length us, event | category | flops | bytes accessed | tf_op | source)
XLA Modules:
  0.0 595.6 jit_solution(7945940527080874917)
XLA Ops:
  8.3 2.3 scatter_fusion.2
  10.6 10.7 %all-to-all-start.2 = ((bf16[64,2,8,512]{3,2,1,0:T(8,128)(2,1)}), bf16[64,2,8,512]{3,2,1,0:T(8,128)(2,1)S(1)}, u32[]{:S(2)}, u32[]{:S(2)}) async-start(bf16[64,2,8,512]{3,2,1,0:T(8,128)(2,1)} %scatter_fusion.2), calls=%async_computation.3 | async-start | bytes 2097152 | tf_op jit(solution)/shard_map/all_to_all | solution.py:99
  21.4 2.5 broadcast_in_dim.73
  23.8 2.3 scatter_fusion
  26.1 23.9 %all-to-all-done.2 = bf16[64,2,8,512]{3,2,1,0:T(8,128)(2,1)S(1)} async-done(((bf16[64,2,8,512]{3,2,1,0:T(8,128)(2,1)}), bf16[64,2,8,512]{3,2,1,0:T(8,128)(2,1)S(1)}, u32[]{:S(2)}, u32[]{:S(2)}) %all-to-all-start.2) | async-done | bytes 1048608 | tf_op jit(solution)/shard_map/all_to_all | solution.py:99
  50.0 5.8 all-to-all-start
  55.9 2.5 bitcast_convert_fusion
  58.5 158.2 %reduce-scatter.2.cloned.1.call-done = f32[2,2,8,512]{3,2,1,0:T(8,128)} async-done(((f32[2,2,512,512]{3,2,1,0:T(8,128)}), f32[2,2,8,512]{3,2,1,0:T(8,128)}) %reduce-scatter.2.cloned.1.call-update) | async-done | bytes 65552 | tf_op jit(solution)/shard_map/reduce_scatter | solution.py:56
  218.2 97.7 %psum.7 = f32[]{:T(128)} all-reduce(f32[]{:T(128)} %multiply_reduce_fusion), channel_id=1, replica_groups=mesh['dp'=64,'mp'=8] {'dp','mp'}, use_global_device_ids=true, to_apply=%region_2.0 | all-reduce | flops 1 | bytes 8 | tf_op jit(solution)/shard_map/psum | solution.py:61
  320.8 8.5 %all-to-all-start.1 = ((bf16[64,2,8,512]{3,2,1,0:T(8,128)(2,1)}), bf16[64,2,8,512]{3,2,1,0:T(8,128)(2,1)S(1)}, u32[]{:S(2)}, u32[]{:S(2)}) async-start(bf16[64,2,8,512]{3,2,1,0:T(8,128)(2,1)} %scatter_fusion.1), calls=%async_computation.2 | async-start | bytes 2097152 | tf_op jit(solution)/shard_map/all_to_all | solution.py:97
  329.4 4.7 copy_bitcast_fusion
  334.1 24.0 %all-to-all-done.1 = bf16[64,2,8,512]{3,2,1,0:T(8,128)(2,1)S(1)} async-done(((bf16[64,2,8,512]{3,2,1,0:T(8,128)(2,1)}), bf16[64,2,8,512]{3,2,1,0:T(8,128)(2,1)S(1)}, u32[]{:S(2)}, u32[]{:S(2)}) %all-to-all-start.1) | async-done | bytes 1048608 | tf_op jit(solution)/shard_map/all_to_all | solution.py:97
  359.2 48.8 %while.12 = (s32[]{:T(128)}, bf16[2,512,512]{2,1,0:T(8,128)(2,1)}, bf16[2,512,1024]{1,2,0:T(8,128)(2,1)}, bf16[2,512,2048]{2,1,0:T(8,128)(2,1)}, bf16[2,512,512]...) while((s32[]{:T(128)}, bf16[2,512,512]{2,1,0:T(8,128)(2,1)}, ...), condition=%wide.region_9.10_spmd, body=%wide.region_6.9_spmd.sunk | while | flops 3768058368 | bytes 61874028 | solution.py:112
  361.3 2.5 copy.65
  370.7 2.6 fusion.115
  383.6 2.1 constant_dynamic-slice_fusion.2
  385.7 2.5 copy.65
  395.2 2.6 fusion.115
  492.3 5.9 all-to-all-start.3
  498.2 6.3 %copy.47 = bf16[2,512,1024]{2,0,1:T(2,128)(2,1)} copy(bf16[2,512,1024]{1,2,0:T(8,128)(2,1)} %get-tuple-element.36) | data formatting | bytes 4194304 | tf_op jit(solution)/shard_map/while | solution.py:112
  504.5 22.5 %all-to-all-done.3 = bf16[64,1,2,8,512]{4,3,2,1,0:T(8,128)(2,1)S(1)} async-done(((bf16[64,1,2,8,512]{4,3,2,1,0:T(8,128)(2,1)}), bf16[64,1,2,8,512]{4,3,2,1,0:T(8,128)(2,1)S(1)}, u32[]{:S(2)}, u32[]{:S(2)}) %all-to-all-start.3) | async-done | bytes 1048608 | tf_op jit(solution)/shard_map/all_to_all | solution.py:115
  527.0 5.7 all-to-all-start.4
  534.2 49.8 %all-to-all-done.4 = bf16[1,2,512,1024]{3,1,0,2:T(2,128)(2,1)S(1)} async-done(((bf16[1,2,512,1024]{3,1,0,2:T(2,128)(2,1)}), bf16[1,2,512,1024]{3,1,0,2:T(2,128)(2,1)S(1)}, u32[]{:S(2)}, u32[]{:S(2)}) %all-to-all-start.4) | async-done | bytes 2097184 | tf_op jit(solution)/shard_map/all_to_all | solution.py:117
  585.9 2.2 gather_fusion.1
  (150 shorter events, 130.0 us)
Async XLA Ops:
  7.2 14.2 %copy-start.9 = (bf16[1,8,8,1024]{3,2,1,0:T(8,128)(2,1)S(1)}, bf16[1,8,8,1024]{3,2,1,0:T(8,128)(2,1)}, u32[]{:S(2)}) copy-start(bf16[1,8,8,1024]{3,2,1,0:T(8,128)(2,1)} %param.20) | copy-start | bytes 393220
  7.2 14.2 %copy-start.10 = (bf16[1,8,8,1024]{3,2,1,0:T(8,128)(2,1)S(1)}, bf16[1,8,8,1024]{3,2,1,0:T(8,128)(2,1)}, u32[]{:S(2)}) copy-start(bf16[1,8,8,1024]{3,2,1,0:T(8,128)(2,1)} %param.21) | copy-start | bytes 393220
  10.6 39.5 %all-to-all-start.2 = ((bf16[64,2,8,512]{3,2,1,0:T(8,128)(2,1)}), bf16[64,2,8,512]{3,2,1,0:T(8,128)(2,1)S(1)}, u32[]{:S(2)}, u32[]{:S(2)}) async-start(bf16[64,2,8,512]{3,2,1,0:T(8,128)(2,1)} %scatter_fusion.2), calls=%async_computation.3 | async-start | bytes 2097152 | tf_op jit(solution)/shard_map/all_to_all | solution.py:99
  21.4 2.5 copy-start.8
  26.1 29.8 %copy-start.1 = (bf16[1,2,2,512,512]{4,3,2,1,0:T(8,128)(2,1)S(1)}, bf16[1,2,2,512,512]{4,3,2,1,0:T(8,128)(2,1)}, u32[]{:S(2)}) copy-start(bf16[1,2,2,512,512]{4,3,2,1,0:T(8,128)(2,1)} %param.19) | copy-start | bytes 6291460
  50.0 270.8 %all-to-all-start = ((bf16[64,2,8,2048]{3,2,1,0:T(8,128)(2,1)}), bf16[64,2,8,2048]{3,2,1,0:T(8,128)(2,1)}, u32[]{:S(2)}, u32[]{:S(2)}) async-start(bf16[64,2,8,2048]{3,2,1,0:T(8,128)(2,1)} %scatter_fusion), calls=%async_computation | async-start | bytes 8388608 | tf_op jit(solution)/shard_map/all_to_all | solution.py:98
  55.9 160.8 %reduce-scatter.2.cloned.1.call-start = ((), (), s32[]{:S(2)}) async-start(), calls=%async_computation.6 | async-start | bytes 4259840 | tf_op jit(solution)/shard_map/reduce_scatter | solution.py:56
  58.5 258.9 %copy-start.11 = (s32[1,4]{1,0:T(1,128)S(1)}, s32[1,4]{1,0:T(1,128)}, u32[]{:S(2)}) copy-start(s32[1,4]{1,0:T(1,128)} %param.23) | copy-start | bytes 52
  320.8 37.3 %all-to-all-start.1 = ((bf16[64,2,8,512]{3,2,1,0:T(8,128)(2,1)}), bf16[64,2,8,512]{3,2,1,0:T(8,128)(2,1)S(1)}, u32[]{:S(2)}, u32[]{:S(2)}) async-start(bf16[64,2,8,512]{3,2,1,0:T(8,128)(2,1)} %scatter_fusion.1), calls=%async_computation.2 | async-start | bytes 2097152 | tf_op jit(solution)/shard_map/all_to_all | solution.py:97
  359.2 4.6 copy-start.4
  365.7 1.2 copy-start.6
  375.0 2.6 copy-start
  377.5 1.6 copy-start.7
  377.5 3.2 copy-start.2
  380.7 2.9 copy-start.5
  382.6 1.0 copy-start.3
  383.6 4.6 copy-start.4
  390.2 1.2 copy-start.6
  399.4 2.6 copy-start
  401.9 1.6 copy-start.7
  402.0 3.2 copy-start.2
  405.1 2.9 copy-start.5
  492.3 34.7 %all-to-all-start.3 = ((bf16[64,1,2,8,512]{4,3,2,1,0:T(8,128)(2,1)}), bf16[64,1,2,8,512]{4,3,2,1,0:T(8,128)(2,1)S(1)}, u32[]{:S(2)}, u32[]{:S(2)}) async-start(bf16[64,1,2,8,512]{4,3,2,1,0:T(8,128)(2,1)} %constant_dynamic-update-slice_fusion), calls=%async_computation.4 | async-start | bytes 2097152 | tf_op jit(solution)/shard_map/all_to_all | solution.py:115
  527.0 56.9 %all-to-all-start.4 = ((bf16[1,2,512,1024]{3,1,0,2:T(2,128)(2,1)}), bf16[1,2,512,1024]{3,1,0,2:T(2,128)(2,1)S(1)}, u32[]{:S(2)}, u32[]{:S(2)}) async-start(bf16[1,2,512,1024]{3,1,0,2:T(2,128)(2,1)} %bitcast.88), calls=%async_computation.5 | async-start | bytes 4194304 | tf_op jit(solution)/shard_map/all_to_all | solution.py:117
  (1 other events, 1.0 us)
Sparse Core Ops, SparseCore 0:
  61.4 155.2 reduce-scatter.1
